TPU v7x, 256 devices: a whole 4x4x8 slice. The times are simulated.
256 devices in a mesh: blk: 32 (over z, y), feat: 8 (over x, core).
Axes of the slice: x: 4, y: 4, z: 8, core: 2. Of those that a mesh axis runs over, the one named last changes fastest.
Arguments:
- features: bfloat16 [262144, 256], P('blk', 'feat'), may hold values from -6 to 6
- tile_cols: int32 [2048, 16], P('blk'), may hold values from 0 to 2047, as said below
- tile_count: int32 [2048], P('blk'), may hold values from 1 to 16, as said below
- edge_mask: int32 [2048, 16, 128, 128], P('blk'), may hold values 0 or 1
- weight: bfloat16 [256, 256], replicated, may hold values from -0.375 to 0.375
- bias: float32 [256], replicated, may hold values from -3 to 3
Outputs:
- result: bfloat16 [262144, 256], P(('blk', 'feat'))
Inputs may be any that keep to these rules, and one draw needn't show every extreme that they name: `tile_cols`: the slots of a row name distinct column blocks. A block c lies with owner c // 64; every column block of row b has an owner within 2 of b // 64, counted cyclically over the blk axis, and among the slots in use of every row one is exactly 2 away. `tile_count`: some block row uses all 16 slots.
All inputs are finite; a program needn't handle non-finite values. Where the computation divides by a largest or mean magnitude, that divisor is 1e-20 or more. No bound on the sum of `edge_mask` on one device may be relied on, other than what follows from the above.
Results may differ from a plain program's by a relative error of at most 0.0075.
Values may be sent and summed in bfloat16 or wider, within the bound.
A program may use at most 192 MiB of HBM per device.

v0:
```python
import jax
import jax.numpy as jnp
from jax import lax
from jax.sharding import PartitionSpec as P

TILE = 128
REACH = 2


epsilon = 1e-06


def shifted(block, axis, distance):
    devices = range(lax.axis_size(axis))
    route = [((i - distance) % len(devices), i) for i in devices]
    return lax.ppermute(block, axis, route)


def normalize(values, peak_abs, blocks_here):
    rows_here = values.shape[0]
    shaped = values.astype(jnp.float32).reshape(
        blocks_here, rows_here // blocks_here, values.shape[1]
    )
    return (shaped / (peak_abs + epsilon)[:, None, None]).astype(jnp.bfloat16).reshape(values.shape)


def finish(mixed, bias):
    return jax.nn.relu(mixed + bias).astype(jnp.bfloat16)


def direct_panel(scaled, offset):
    return shifted(scaled, "blk", -offset)


def per_device(features, tile_cols, tile_count, edge_mask, weight, bias):
    row_total, feat_part = features.shape
    block_rows = tile_cols.shape[0]
    slot_total = tile_cols.shape[1]
    slot_ids = jnp.arange(slot_total, dtype=jnp.int32)
    active = slot_ids[None, :] < tile_count[:, None]
    row_ones = jnp.sum(edge_mask, axis=3)
    degree = jnp.sum(jnp.where(active[:, :, None], row_ones, 0), axis=1).reshape(row_total) + 1
    inv_root = lax.rsqrt(degree.astype(jnp.float32))
    scaled = (features.astype(jnp.float32) * inv_root[:, None]).astype(jnp.bfloat16)
    pieces = []
    for offset in range(-REACH, REACH + 1):
        pieces.append(scaled if offset == 0 else direct_panel(scaled, offset))
    nearby = jnp.concatenate(pieces, axis=0)
    near_blocks = nearby.reshape(nearby.shape[0] // TILE, TILE, feat_part)
    owner_here = lax.axis_index("blk")
    cycle_size = lax.axis_size("blk")
    distance = (tile_cols // block_rows - owner_here + REACH) % cycle_size
    local_index = distance * block_rows + tile_cols % block_rows
    picked = near_blocks[local_index]
    weighted = jnp.where(active[:, :, None, None], edge_mask, 0).astype(jnp.bfloat16)
    summed = jnp.einsum("btij,btjf->bif", weighted, picked, preferred_element_type=jnp.float32)
    summed = summed + scaled.reshape(block_rows, TILE, feat_part).astype(jnp.float32)
    aggregate = (summed.reshape(row_total, feat_part) * inv_root[:, None]).astype(jnp.bfloat16)
    local_peak = jnp.max(
        jnp.abs(aggregate.astype(jnp.float32)).reshape(block_rows, TILE * feat_part), axis=1
    )
    peak_abs = lax.pmax(local_peak, "feat")
    normalized = normalize(aggregate, peak_abs, block_rows)
    owned = lax.all_to_all(normalized, "feat", split_axis=0, concat_axis=1, tiled=True)
    mixed = jnp.dot(owned, weight, preferred_element_type=jnp.float32)
    return finish(mixed, bias)


def solution(mesh):
    placed = (P("blk", "feat"), P("blk", None), P("blk"), P("blk", None, None, None), P(), P())
    return jax.shard_map(
        per_device, mesh=mesh, in_specs=placed, out_specs=P(("blk", "feat"), None), check_vma=False
    )
```

profile of v0, /device:TPU:152, one launch (start us, length us, event | category | flops | bytes accessed | tf_op | source)
XLA Modules:
  0.0 139.2 jit_solution(7088539412983430475)
XLA Ops:
  0.0 0.0 copy-start
  0.0 0.8 iota_compare_fusion
  0.8 0.0 copy-start.1
  0.8 21.6 %reduce_sum.18 = s32[64,16,128]{2,1,0:T(8,128)S(1)} reduce(s32[64,16,128,128]{3,2,1,0:T(8,128)} %param.9, s32[]{:T(128)} %constant.45.clone.1), dimensions={3}, to_apply=%region_0.0 | reduce | flops 16646144 | bytes 67633152 | tf_op jit(solution)/shard_map/reduce_sum | solution.py:41
  22.4 0.0 copy-start.2
  22.4 0.2 select_reduce_fusion
  22.7 0.0 copy-done.1
  22.7 1.2 convert_bitcast_fusion
  23.9 1.7 %collective-permute-start = (bf16[8192,32]{0,1:T(8,128)(2,1)S(1)}, bf16[8192,32]{0,1:T(8,128)(2,1)S(1)}, u32[]{:S(2)}, u32[]{:S(2)}) collective-permute-start(bf16[8192,32]{0,1:T(8,128)(2,1)S(1)} %get-tuple-element.6), channel_id=1, source_target_pairs={{240,0},{248,8},{0,16},{8,24},{16,32},{24,40},{32,48},{40,56},{48,... | collective-permute-start | bytes 1572872 | tf_op jit(solution)/shard_map/ppermute | solution.py:16
  25.6 1.8 %collective-permute-start.3 = (bf16[8192,32]{0,1:T(8,128)(2,1)S(1)}, bf16[8192,32]{0,1:T(8,128)(2,1)S(1)}, u32[]{:S(2)}, u32[]{:S(2)}) collective-permute-start(bf16[8192,32]{0,1:T(8,128)(2,1)S(1)} %get-tuple-element.6), channel_id=1, source_target_pairs={{16,0},{24,8},{32,16},{40,24},{48,32},{56,40},{64,48},{72,56},{80,... | collective-permute-start | bytes 1572872 | tf_op jit(solution)/shard_map/ppermute | solution.py:16
  27.4 0.7 collective-permute-start.2
  28.2 3.4 %collective-permute-start.1 = (bf16[8192,32]{0,1:T(8,128)(2,1)S(1)}, bf16[8192,32]{0,1:T(8,128)(2,1)S(1)}, u32[]{:S(2)}, u32[]{:S(2)}) collective-permute-start(bf16[8192,32]{0,1:T(8,128)(2,1)S(1)} %get-tuple-element.6), channel_id=1, source_target_pairs={{248,0},{0,8},{8,16},{16,24},{24,32},{32,40},{40,48},{48,56},{56,6... | collective-permute-start | bytes 1572872 | tf_op jit(solution)/shard_map/ppermute | solution.py:16
  31.6 0.0 copy-done.2
  31.6 0.1 copy.22
  31.7 0.1 reshape.81
  31.8 29.1 %collective-permute-done = bf16[8192,32]{0,1:T(8,128)(2,1)S(1)} collective-permute-done((bf16[8192,32]{0,1:T(8,128)(2,1)S(1)}, bf16[8192,32]{0,1:T(8,128)(2,1)S(1)}, u32[]{:S(2)}, u32[]{:S(2)}) %collective-permute-start) | collective-permute-done | bytes 524320 | tf_op jit(solution)/shard_map/ppermute | solution.py:16
  60.9 11.5 %collective-permute-done.1 = bf16[8192,32]{0,1:T(8,128)(2,1)S(1)} collective-permute-done((bf16[8192,32]{0,1:T(8,128)(2,1)S(1)}, bf16[8192,32]{0,1:T(8,128)(2,1)S(1)}, u32[]{:S(2)}, u32[]{:S(2)}) %collective-permute-start.1) | collective-permute-done | bytes 524320 | tf_op jit(solution)/shard_map/ppermute | solution.py:16
  72.4 0.0 collective-permute-done.2
  72.5 0.0 collective-permute-done.3
  72.6 0.5 copy_bitcast_fusion
  73.0 9.9 %gather_fusion = bf16[1024,128,32]{1,2,0:T(8,128)(2,1)} fusion(bf16[320,128,32]{1,2,0:T(8,128)(2,1)S(1)} %copy_bitcast_fusion, s32[1024]{0:T(1024)S(1)} %broadcast_clamp_fusion), kind=kCustom, calls=%fused_computation | custom fusion | bytes 16781312 | tf_op jit(solution)/shard_map/gather | solution.py:54
  82.9 26.6 %fusion.9 = (f32[64]{0:T(128)S(1)}, bf16[64,128,32]{1,2,0:T(8,128)(2,1)S(1)}) fusion(f32[64,128]{1,0:T(8,128)S(1)} %get-tuple-element.7, f32[4,64,8,128]{3,2,1,0:T(8,128)} %get-tuple-element.5, bf16[64,16,128,32]{2,3,1,0:T(8,128)(2,1)} %bitcast.29, s32[64,16,128,128]{3,2,1,0:T(8,128)} %param.9, pred[64,16]{1,0:T(8,128)(4,1)S(1)} %iota_compare_fusion), kind=kOutput, calls=%fused_computation.15 | convolution fusion | flops 1108869120 | bytes 77104384 | tf_op jit(solution)/shard_map/btij,btjf->bif/dot_general | solution.py:56
  109.5 14.8 %pmax.7 = f32[64]{0:T(128)S(1)} all-reduce(f32[64]{0:T(128)S(1)} %get-tuple-element.9), channel_id=1, replica_groups=mesh['blk'=32,'feat'=8] {'feat'}, use_global_device_ids=true, to_apply=%region_3.4 | all-reduce | flops 64 | bytes 512 | tf_op jit(solution)/shard_map/pmax | solution.py:62
  124.3 0.0 copy-start.3
  124.3 0.2 fusion.10
  124.5 0.2 copy.25
  124.7 0.2 all_to_all.14
  124.9 0.3 copy.26
  125.2 12.8 %all_to_all.19 = bf16[8,1024,32]{1,2,0:T(8,128)(2,1)S(1)} all-to-all(bf16[8,1024,32]{1,2,0:T(8,128)(2,1)S(1)} %copy.26), channel_id=1, replica_groups=mesh['blk'=32,'feat'=8] {'feat'}, dimensions={0} | all-to-all | bytes 1048576 | tf_op jit(solution)/shard_map/all_to_all | solution.py:64
  138.0 0.0 copy-done
  138.0 0.0 copy-done.3
  138.0 1.1 fusion.7
  (9 shorter events, 0.2 us)
Async XLA Ops:
  0.0 138.0 %copy-start = (bf16[256,256]{1,0:T(8,128)(2,1)S(1)}, bf16[256,256]{1,0:T(8,128)(2,1)}, u32[]{:S(2)}) copy-start(bf16[256,256]{1,0:T(8,128)(2,1)} %param.10) | copy-start | bytes 393220
  0.8 21.9 %copy-start.1 = (bf16[8192,32]{0,1:T(8,128)(2,1)S(1)}, bf16[8192,32]{0,1:T(8,128)(2,1)}, u32[]{:S(2)}) copy-start(bf16[8192,32]{0,1:T(8,128)(2,1)} %param.6) | copy-start | bytes 1572868
  22.4 9.1 %copy-start.2 = (s32[64,16]{0,1:T(8,128)S(1)}, s32[64,16]{0,1:T(8,128)}, u32[]{:S(2)}) copy-start(s32[64,16]{0,1:T(8,128)} %param.7) | copy-start | bytes 12292
  23.9 36.9 %collective-permute-start = (bf16[8192,32]{0,1:T(8,128)(2,1)S(1)}, bf16[8192,32]{0,1:T(8,128)(2,1)S(1)}, u32[]{:S(2)}, u32[]{:S(2)}) collective-permute-start(bf16[8192,32]{0,1:T(8,128)(2,1)S(1)} %get-tuple-element.6), channel_id=1, source_target_pairs={{240,0},{248,8},{0,16},{8,24},{16,32},{24,40},{32,48},{40,56},{48,... | collective-permute-start | bytes 1572872 | tf_op jit(solution)/shard_map/ppermute | solution.py:16
  25.6 46.9 %collective-permute-start.3 = (bf16[8192,32]{0,1:T(8,128)(2,1)S(1)}, bf16[8192,32]{0,1:T(8,128)(2,1)S(1)}, u32[]{:S(2)}, u32[]{:S(2)}) collective-permute-start(bf16[8192,32]{0,1:T(8,128)(2,1)S(1)} %get-tuple-element.6), channel_id=1, source_target_pairs={{16,0},{24,8},{32,16},{40,24},{48,32},{56,40},{64,48},{72,56},{80,... | collective-permute-start | bytes 1572872 | tf_op jit(solution)/shard_map/ppermute | solution.py:16
  27.4 45.0 %collective-permute-start.2 = (bf16[8192,32]{0,1:T(8,128)(2,1)S(1)}, bf16[8192,32]{0,1:T(8,128)(2,1)S(1)}, u32[]{:S(2)}, u32[]{:S(2)}) collective-permute-start(bf16[8192,32]{0,1:T(8,128)(2,1)S(1)} %get-tuple-element.6), channel_id=1, source_target_pairs={{8,0},{16,8},{24,16},{32,24},{40,32},{48,40},{56,48},{64,56},{72,6... | collective-permute-start | bytes 1572872 | tf_op jit(solution)/shard_map/ppermute | solution.py:16
  28.2 44.2 %collective-permute-start.1 = (bf16[8192,32]{0,1:T(8,128)(2,1)S(1)}, bf16[8192,32]{0,1:T(8,128)(2,1)S(1)}, u32[]{:S(2)}, u32[]{:S(2)}) collective-permute-start(bf16[8192,32]{0,1:T(8,128)(2,1)S(1)} %get-tuple-element.6), channel_id=1, source_target_pairs={{248,0},{0,8},{8,16},{16,24},{24,32},{32,40},{40,48},{48,56},{56,6... | collective-permute-start | bytes 1572872 | tf_op jit(solution)/shard_map/ppermute | solution.py:16
  124.3 13.8 %copy-start.3 = (f32[256]{0:T(256)S(1)}, f32[256]{0:T(256)}, u32[]{:S(2)}) copy-start(f32[256]{0:T(256)} %param.11) | copy-start | bytes 3076
where the time goes:
time: 139 us
  waiting for transfers between devices  40.6 us (29%)
  matrix products  27.7 us (20%)
  blocking collectives  27.6 us (20%)
  other arithmetic  24 us (17%)
  local copies, waits for them, and re-layouts  11.4 us (8%)
  starting transfers between devices  7.67 us (6%)
    ppermute x4, waiting for transfers between devices, shifted(): return lax.ppermute(block, axis, route)  40.6 us
    dot_general x1, matrix products, per_device(): jnp.einsum('btij,btjf->bif', weighted, picked, preferred_element_type=jnp...  26.6 us
    reduce_sum x1, other arithmetic, per_device(): row_ones = jnp.sum(edge_mask, axis=3)  21.6 us
    pmax x1, blocking collectives, per_device(): peak_abs = lax.pmax(local_peak, 'feat')  14.8 us
    all_to_all x1, blocking collectives, per_device(): lax.all_to_all(normalized, 'feat', split_axis=0, concat_axis=1, tiled=True)  12.8 us
    gather x1, local copies, waits for them, and re-layouts, per_device(): picked = near_blocks[local_index]  9.88 us
    ppermute x4, starting transfers between devices, shifted(): return lax.ppermute(block, axis, route)  7.67 us
  transfers between devices with their start and end apart: 4, of which 2 were waited for; matrix products, arithmetic and copies ran while one was open for 0% of the time, Pallas kernels for 0%

commit v1 on v0

v1 whole, which is shorter than its diff:
```python
import functools

import jax
import jax.numpy as jnp
from jax import lax
from jax.experimental import pallas as pl
from jax.experimental.pallas import tpu as pltpu
from jax.sharding import PartitionSpec as P

MESH = pl.DeviceIdType.MESH

TILE = 128
REACH = 2
SPAN = 2 * REACH + 1
epsilon = 1e-06

CORES = 2
ROWS = 64
SLOTS = 16
PART = 32
WIDE = CORES * PART
HALF = ROWS // CORES
GROUP = 8
CHIPS = 4
STAGES = 16
NODES = ROWS * TILE

NT = (((1,), (1,)), ((), ()))
TN = (((0,), (0,)), ((), ()))


def kernel(
    ft, mask, idx, count, weight, bias, out,
    stage, tiles, raw, scaled, inv, degq, degall, aggsend, aggrecv,
    stage_sem, own_sem, panel_send, panel_recv, pair_send, pair_recv,
    degq_send, degq_recv, degall_send, degall_recv, agg_send, agg_recv,
):
    blk = lax.axis_index("blk")
    feat = lax.axis_index("feat")
    owners = lax.axis_size("blk")
    feats = lax.axis_size("feat")
    chip, core = feat // CORES, feat % CORES
    partner = (blk, chip * CORES + 1 - core)

    def owner(d):
        return lax.rem(blk + d + owners, owners)

    def block_row(q):
        j, k = q // GROUP, q % GROUP
        return lax.rem(chip + j, CHIPS) * (CORES * GROUP) + core * GROUP + k

    def stage_copy(q):
        slot = q % STAGES
        return pltpu.make_async_copy(mask.at[block_row(q)], stage.at[slot], stage_sem.at[slot])

    for q in range(STAGES):
        stage_copy(q).start()
    own_copy = pltpu.make_async_copy(ft, raw.at[core, REACH], own_sem)
    own_copy.start()
    scaled[SPAN * ROWS] = jnp.zeros((WIDE, TILE), jnp.bfloat16)

    barrier = pltpu.get_barrier_semaphore()
    offsets = [d for d in range(-REACH, REACH + 1) if d != 0]
    for d in offsets:
        pl.semaphore_signal(barrier, inc=1, device_id=(owner(d), feat), device_id_type=MESH)
    for s in range(1, feats):
        pl.semaphore_signal(barrier, inc=1, device_id=(blk, lax.rem(feat + s, feats)), device_id_type=MESH)
    pl.semaphore_wait(barrier, len(offsets) + feats - 1)

    def panel_copy(d):
        return pltpu.make_async_remote_copy(
            src_ref=ft, dst_ref=raw.at[core, REACH - d],
            send_sem=panel_send.at[REACH - d], recv_sem=panel_recv.at[REACH - d],
            device_id=(owner(d), feat), device_id_type=MESH)

    def pair_copy(slot):
        return pltpu.make_async_remote_copy(
            src_ref=ft if slot == REACH else raw.at[core, slot], dst_ref=raw.at[core, slot],
            send_sem=pair_send.at[slot], recv_sem=pair_recv.at[slot],
            device_id=partner, device_id_type=MESH)

    for d in (-2, 2, -1, 1):
        panel_copy(d).start()
    pair_copy(REACH).start()

    def convert(q):
        slot = q % STAGES
        stage_copy(q).wait()
        for t in range(SLOTS):
            tiles[q, :, t * TILE:(t + 1) * TILE] = stage[slot, t].astype(jnp.float32).astype(jnp.bfloat16)

    def own_row(q, _):
        convert(q)
        b = block_row(q)
        n = count[b]
        total = jnp.zeros((TILE, TILE), jnp.int32)
        for t in range(SLOTS):
            total = total + stage[q, t] * (t < n).astype(jnp.int32)
        total = total.astype(jnp.float32).astype(jnp.bfloat16)
        ones = jnp.ones((8, TILE), jnp.bfloat16)
        degree = 1.0 + lax.dot_general(ones, total, NT, preferred_element_type=jnp.float32)
        degq[REACH, pl.ds(q, 1)] = degree[0:1]
        stage_copy(q + STAGES).start()
        return 0

    lax.fori_loop(0, GROUP, own_row, 0)

    def degq_copy(d):
        return pltpu.make_async_remote_copy(
            src_ref=degq.at[REACH], dst_ref=degq.at[REACH - d],
            send_sem=degq_send.at[REACH - d], recv_sem=degq_recv.at[REACH - d],
            device_id=(owner(d), feat), device_id_type=MESH)

    def degall_copy(s):
        return pltpu.make_async_remote_copy(
            src_ref=degq, dst_ref=degall.at[feat],
            send_sem=degall_send.at[s], recv_sem=degall_recv.at[s],
            device_id=(blk, lax.rem(feat + s, feats)), device_id_type=MESH)

    for d in offsets:
        degq_copy(d).start()

    def more_rows(q, _):
        convert(q)

        @pl.when(q < HALF - STAGES)
        def _():
            stage_copy(q + STAGES).start()
        return 0

    lax.fori_loop(GROUP, STAGES, more_rows, 0)

    for d in offsets:
        degq_copy(d).wait()
    for s in range(1, feats):
        degall_copy(s).start()
    degall[feat] = degq[...]

    lax.fori_loop(STAGES, HALF, more_rows, 0)

    for s in range(1, feats):
        degall_copy(s).wait()
    for f in range(feats):
        for d in range(SPAN):
            inv[pl.ds(d * ROWS + f * GROUP, GROUP)] = lax.rsqrt(degall[f, d])

    own_copy.wait()
    pair_copy(REACH).wait()

    def scale(slot):
        def body(c, _):
            at = pl.multiple_of(c * TILE, TILE)
            row = slot * ROWS + c
            factor = inv[pl.ds(row, 1)]
            for h in range(CORES):
                block = raw[h, slot, :, pl.ds(at, TILE)].astype(jnp.float32)
                scaled[row, h * PART:(h + 1) * PART] = (block * factor).astype(jnp.bfloat16)
            return 0
        lax.fori_loop(0, ROWS, body, 0, unroll=4)

    scale(REACH)
    for d in (-1, 1, -2, 2):
        slot = REACH + d
        panel_copy(-d).wait()
        pair_copy(slot).start()
    for d in (-1, 1, -2, 2):
        slot = REACH + d
        pair_copy(slot).wait()
        scale(slot)

    def agg_copy(j):
        return pltpu.make_async_remote_copy(
            src_ref=aggsend.at[j], dst_ref=aggrecv.at[:, pl.ds(pl.multiple_of(chip * WIDE, WIDE), WIDE)],
            send_sem=agg_send.at[j], recv_sem=agg_recv.at[j],
            device_id=(blk, lax.rem(chip + j, CHIPS) * CORES + core), device_id_type=MESH)

    def aggregate(q):
        b = block_row(q)
        total = jnp.zeros((WIDE, TILE), jnp.float32)
        for pair in range(SLOTS // 2):
            left = jnp.concatenate(
                [scaled[idx[b, 2 * pair]], scaled[idx[b, 2 * pair + 1]]], axis=1)
            right = tiles[q, :, pair * 2 * TILE:(pair + 1) * 2 * TILE]
            total = total + lax.dot_general(left, right, NT, preferred_element_type=jnp.float32)
        total = total + scaled[REACH * ROWS + b].astype(jnp.float32)
        return (total * inv[pl.ds(REACH * ROWS + b, 1)]).astype(jnp.bfloat16)

    for j in (2, 1, 3):
        def send_row(k, _, j=j):
            aggsend[j, k] = aggregate(j * GROUP + k)
            return 0
        lax.fori_loop(0, GROUP, send_row, 0)
        agg_copy(j).start()

    def keep_row(k, _):
        aggrecv[k, pl.ds(pl.multiple_of(chip * WIDE, WIDE), WIDE)] = aggregate(k)
        return 0
    lax.fori_loop(0, GROUP, keep_row, 0)

    for j in (2, 1, 3):
        agg_copy(j).wait()

    def finish(k, _):
        values = aggrecv[k].astype(jnp.float32)
        peak_abs = jnp.max(jnp.abs(values))
        normalized = (values / (peak_abs + epsilon)).astype(jnp.bfloat16)
        mixed = lax.dot_general(normalized, weight[...], TN, preferred_element_type=jnp.float32)
        mixed = jnp.maximum(mixed + bias[...], 0.0).astype(jnp.bfloat16)
        out[pl.ds(pl.multiple_of(k * TILE, TILE), TILE)] = mixed
        return 0
    lax.fori_loop(0, GROUP, finish, 0)


def per_device(features, tile_cols, tile_count, edge_mask, weight, bias):
    slot_ids = jnp.arange(SLOTS, dtype=jnp.int32)
    active = slot_ids[None, :] < tile_count[:, None]
    owners = lax.axis_size("blk")
    distance = (tile_cols // ROWS - lax.axis_index("blk") + REACH) % owners
    idx = jnp.where(active, distance * ROWS + tile_cols % ROWS, SPAN * ROWS)
    feats = lax.axis_size("feat")
    smem = pl.BlockSpec(memory_space=pltpu.SMEM)
    vmem = pl.BlockSpec(memory_space=pltpu.VMEM)
    hbm = pl.BlockSpec(memory_space=pl.ANY)
    dma = pltpu.SemaphoreType.DMA
    return pl.pallas_call(
        kernel,
        out_shape=jax.ShapeDtypeStruct((GROUP * TILE, weight.shape[1]), jnp.bfloat16),
        in_specs=[hbm, hbm, smem, smem, vmem, vmem],
        out_specs=vmem,
        scratch_shapes=[
            pltpu.VMEM((STAGES, SLOTS, TILE, TILE), jnp.int32),
            pltpu.VMEM((HALF, TILE, SLOTS * TILE), jnp.bfloat16),
            pltpu.VMEM((CORES, SPAN, PART, NODES), jnp.bfloat16),
            pltpu.VMEM((SPAN * ROWS + 1, WIDE, TILE), jnp.bfloat16),
            pltpu.VMEM((SPAN * ROWS, TILE), jnp.float32),
            pltpu.VMEM((SPAN, GROUP, TILE), jnp.float32),
            pltpu.VMEM((feats, SPAN, GROUP, TILE), jnp.float32),
            pltpu.VMEM((CHIPS, GROUP, WIDE, TILE), jnp.bfloat16),
            pltpu.VMEM((GROUP, CHIPS * WIDE, TILE), jnp.bfloat16),
            dma((STAGES,)), dma, dma((SPAN,)), dma((SPAN,)), dma((SPAN,)), dma((SPAN,)),
            dma((SPAN,)), dma((SPAN,)), dma((feats,)), dma((feats,)), dma((CHIPS,)), dma((CHIPS,)),
        ],
        compiler_params=pltpu.CompilerParams(
            collective_id=0, has_side_effects=True, vmem_limit_bytes=60 * 1024 * 1024),
    )(features.T, edge_mask, idx, tile_count, weight, bias.reshape(1, -1))


def solution(mesh):
    placed = (P("blk", "feat"), P("blk", None), P("blk"), P("blk", None, None, None), P(), P())
    return jax.shard_map(
        per_device, mesh=mesh, in_specs=placed, out_specs=P(("blk", "feat"), None), check_vma=False
    )
```

time: 139 us -> 82.8 us (0.60)
  the two profiles are of different devices: /device:TPU:152 before, /device:TPU:2 now
where the time goes in v1:
time: 82.8 us; the launch traced here: 82 us
  Pallas kernels  78 us (94%)
  local copies, waits for them, and re-layouts  2.65 us (3%)
  other arithmetic  1.35 us (2%)
    pallas_call x1, Pallas kernels, per_device(): pl.pallas_call(kernel, out_shape=jax.ShapeDtypeStruct((GROUP * TILE, weig...  78 us
    unnamed x2, local copies, waits for them, and re-layouts  2.65 us

profile of v1, /device:TPU:2, one launch (start us, length us, event | category | flops | bytes accessed | tf_op | source)
XLA Modules:
  0.0 82.0 jit_solution(16459519963927869175)
XLA Ops:
  0.0 0.8 copy.7
  0.8 1.3 %fusion.5.idx = s32[64,16]{1,0:T(8,128)} fusion(s32[64,16]{1,0:T(8,128)S(1)} %copy.7, s32[]{:T(128)S(6)} %axis_index.15, s32[64]{0:T(128)} %count.1), kind=kLoop, calls=%fused_computation.13 | loop fusion | flops 36864 | bytes 8452 | tf_op jit(solution)/shard_map/jit(_where)/select_n | solution.py:219
  2.1 78.0 %shard_map.64 = bf16[1024,256]{1,0:T(8,128)(2,1)} custom-call(bf16[32,8192]{1,0:T(8,128)(2,1)} %bitcast.2, s32[64,16,128,128]{3,2,1,0:T(8,128)} %mask.1, s32[64,16]{1,0:T(8,128)} %fusion.5.idx, s32[64]{0:T(128)} %count.1, bf16[256,256]{1,0:T(8,128)(2,1)} %weight.1, f32[1,256]{1,0:T(1,128)} %bitcast.3), custom_call_target="tpu_custom_call" | custom-call | tf_op jit(solution)/shard_map/pallas_call | solution.py:225
  80.2 1.9 %copy.12 = bf16[1024,256]{1,0:T(8,128)(2,1)} copy(bf16[1024,256]{1,0:T(8,128)(2,1)} %shard_map.64) | data formatting | bytes 1048576

commit v2 on v1

v2 whole, which is shorter than its diff:
```python
import functools

import jax
import jax.numpy as jnp
from jax import lax
from jax.experimental import pallas as pl
from jax.experimental.pallas import tpu as pltpu
from jax.sharding import PartitionSpec as P

MESH = pl.DeviceIdType.MESH

TILE = 128
REACH = 2
SPAN = 2 * REACH + 1
epsilon = 1e-06

CORES = 2
ROWS = 64
SLOTS = 16
PART = 32
HALVES = 2
SUB = PART // HALVES
WIDE = CORES * SUB
HALF = ROWS // CORES
GROUP = 8
CHIPS = 4
RING = 4
STAGES = 16
NODES = ROWS * TILE

CHUNKS = 4
TOTAL = HALVES * CHUNKS
BLOCKS = ROWS // CHUNKS
LANES = BLOCKS * TILE
CROSS = (3,)
AHEAD = 2
PASS = SPAN
STEPS = TOTAL + 4
PAIRS = 2
SUBS = GROUP // PAIRS

NT = (((1,), (1,)), ((), ()))
TN = (((0,), (0,)), ((), ()))


def crosses(n):
    return n % CHUNKS in CROSS


def kernel(
    ft, mask, cols, count, weight, bias, out,
    stage, tiles, raw, scaled, inv, degq, degall, aggsend, aggrecv, order,
    stage_sem, own_sem, panel_send, panel_recv, pair_send, pair_recv,
    degq_send, degq_recv, degall_send, degall_recv, agg_send, agg_recv,
):
    blk = lax.axis_index("blk")
    feat = lax.axis_index("feat")
    owners = lax.axis_size("blk")
    feats = lax.axis_size("feat")
    layers = owners // RING
    chip, core = feat // CORES, feat % CORES
    z, y = blk // RING, blk % RING

    mirrored = y >= RING // 2
    place = jnp.where(mirrored, RING - 1 - y, y)
    outer = place == 0
    inner = place == 1
    ahead_z = jnp.where(mirrored, layers - 1, 1)

    def at(zz, yy):
        return (zz * RING + yy, feat)

    near = at(z, jnp.where(mirrored, 2 + place, 1 - place))
    across = at(z, RING - 1 - y)
    up = at(lax.rem(z + ahead_z, layers), y)
    down = at(lax.rem(z + layers - ahead_z, layers), y)
    partner = (blk, chip * CORES + 1 - core)

    def owner(d):
        return lax.rem(blk + d + owners, owners)

    def block_row(q):
        j, k = q // GROUP, q % GROUP
        return lax.rem(chip + j, CHIPS) * (CORES * GROUP) + core * GROUP + k

    def stage_copy(q):
        slot = q % STAGES
        return pltpu.make_async_copy(mask.at[block_row(q)], stage.at[slot], stage_sem.at[slot])

    for q in range(STAGES):
        stage_copy(q).start()
    own_copy = pltpu.make_async_copy(ft, raw.at[core, REACH], own_sem)
    own_copy.start()

    barrier = pltpu.get_barrier_semaphore()
    offsets = [d for d in range(-REACH, REACH + 1) if d != 0]
    peers = [near, across, up, down]
    peers += [(owner(d), feat) for d in offsets]
    peers += [(blk, lax.rem(feat + s, feats)) for s in range(1, feats)]
    for peer in peers:
        pl.semaphore_signal(barrier, inc=1, device_id=peer, device_id_type=MESH)
    pl.semaphore_wait(barrier, len(peers))

    def piece(n):
        h, c = n // CHUNKS, n % CHUNKS
        return pl.ds(h * SUB, SUB), pl.ds(c * LANES, LANES)

    def panel_copy(source, target, n, device, kind):
        features, nodes = piece(n)
        src = ft.at[features, nodes] if source == REACH else raw.at[core, source, features, nodes]
        return pltpu.make_async_remote_copy(
            src_ref=src, dst_ref=raw.at[core, target, features, nodes],
            send_sem=panel_send.at[kind, n], recv_sem=panel_recv.at[target, n],
            device_id=device, device_id_type=MESH)

    def pair_copy(slot, n):
        features, nodes = piece(n)
        here = raw.at[core, slot, features, nodes]
        return pltpu.make_async_remote_copy(
            src_ref=ft.at[features, nodes] if slot == REACH else here, dst_ref=here,
            send_sem=pair_send.at[slot, n], recv_sem=pair_recv.at[slot, n],
            device_id=partner, device_id_type=MESH)

    def arrive(slot, n):
        panel_copy(slot, slot, n, near, 0).wait_recv()

    every, far, close = (lambda n: True), crosses, (lambda n: not crosses(n))
    outer_sends = {
        (REACH, 0): (1, near, every), (REACH, 1): (PASS, across, far), (3, 2): (4, across, every),
        (PASS, 3): (4, near, far), (PASS, 4): (1, up, far), (4, 5): (0, up, every)}
    inner_sends = {
        (REACH, 0): (3, near, every), (REACH, 1): (3, across, every), (1, 2): (4, across, close),
        (4, 3): (0, up, every), (0, 4): (1, near, close)}

    def forward(table, source, n, wait=False):
        for (start, kind), (target, device, which) in table.items():
            if start == source and which(n):
                copy = panel_copy(start, target, n, device, kind)
                if wait:
                    copy.wait_send()
                else:
                    copy.start()

    def send_own(n):
        @pl.when(outer)
        def _():
            forward(outer_sends, REACH, n)

        @pl.when(inner)
        def _():
            forward(inner_sends, REACH, n)
        pair_copy(REACH, n).start()

    def relay(table, slot, n):
        arrive(slot, n)
        forward(table, slot, n)
        if slot != PASS:
            pair_copy(slot, n).start()

    def transfer(step):
        a, b, c, d = step, step - 1, step - 2, step - 3

        @pl.when(outer)
        def _():
            if 0 <= d < TOTAL and not crosses(d):
                relay(outer_sends, 1, d)
            if 0 <= c < TOTAL:
                relay(outer_sends, 0, c)
            if 0 <= b < TOTAL:
                relay(outer_sends, 4, b)
                if crosses(b):
                    relay(outer_sends, 1, b)
            if a < TOTAL:
                if crosses(a):
                    relay(outer_sends, PASS, a)
                relay(outer_sends, 3, a)

        @pl.when(inner)
        def _():
            if 0 <= c < TOTAL:
                relay(inner_sends, 0, c)
            if 0 <= b < TOTAL:
                relay(inner_sends, 4, b)
            if a < TOTAL:
                relay(inner_sends, 1, a)
                relay(inner_sends, 3, a)
        if a + AHEAD < TOTAL:
            send_own(a + AHEAD)

    for n in range(AHEAD):
        send_own(n)

    for h in range(HALVES):
        scaled[h, SPAN * ROWS] = jnp.zeros((WIDE, TILE), jnp.bfloat16)
    for x in range(CHIPS):
        for c in range(CORES):
            for h in range(HALVES):
                source = (x * CORES + c) * PART + h * SUB
                target = (h * CHIPS + x) * WIDE + c * SUB
                order[target:target + SUB] = weight[source:source + SUB]

    def convert(q):
        slot = q % STAGES
        stage_copy(q).wait()
        for t in range(SLOTS):
            tiles[q, :, t * TILE:(t + 1) * TILE] = stage[slot, t].astype(jnp.float32).astype(jnp.bfloat16)

    def own_row(q, _):
        convert(q)
        n = count[block_row(q)]
        total = jnp.zeros((TILE, TILE), jnp.int32)
        for t in range(SLOTS):
            total = total + stage[q, t] * (t < n).astype(jnp.int32)
        total = total.astype(jnp.float32).astype(jnp.bfloat16)
        ones = jnp.ones((8, TILE), jnp.bfloat16)
        degree = 1.0 + lax.dot_general(ones, total, NT, preferred_element_type=jnp.float32)
        degq[REACH, pl.ds(q, 1)] = degree[0:1]
        stage_copy(q + STAGES).start()
        return 0

    def more_row(q, _):
        convert(q)

        @pl.when(q < HALF - STAGES)
        def _():
            stage_copy(q + STAGES).start()
        return 0

    def degq_copy(d):
        return pltpu.make_async_remote_copy(
            src_ref=degq.at[REACH], dst_ref=degq.at[REACH - d],
            send_sem=degq_send.at[REACH - d], recv_sem=degq_recv.at[REACH - d],
            device_id=(owner(d), feat), device_id_type=MESH)

    def degall_copy(s):
        return pltpu.make_async_remote_copy(
            src_ref=degq, dst_ref=degall.at[feat],
            send_sem=degall_send.at[s], recv_sem=degall_recv.at[s],
            device_id=(blk, lax.rem(feat + s, feats)), device_id_type=MESH)

    def scale(n):
        h, c = n // CHUNKS, n % CHUNKS
        for slot in range(SPAN):
            pair_copy(slot, n).wait()
        for slot in range(SPAN):
            there = jnp.where(mirrored, SPAN - 1 - slot, slot) * ROWS

            def body(i, _, slot=slot, there=there):
                block = c * BLOCKS + i
                nodes = pl.ds(pl.multiple_of(block * TILE, TILE), TILE)
                factor = inv[pl.ds(there + block, 1)]
                for k in range(CORES):
                    values = raw[k, slot, h * SUB:(h + 1) * SUB, nodes].astype(jnp.float32)
                    scaled[h, there + block, k * SUB:(k + 1) * SUB] = (values * factor).astype(jnp.bfloat16)
                return 0
            lax.fori_loop(0, BLOCKS, body, 0, unroll=4)

    def agg_copy(h, j, s):
        rows = pl.ds(s * PAIRS, PAIRS)
        return pltpu.make_async_remote_copy(
            src_ref=aggsend.at[h, j, rows], dst_ref=aggrecv.at[rows, h, chip],
            send_sem=agg_send.at[h, j, s], recv_sem=agg_recv.at[h, j, s],
            device_id=(blk, lax.rem(chip + j, CHIPS) * CORES + core), device_id_type=MESH)

    first = (blk - REACH) * ROWS
    blocks = owners * ROWS

    def aggregate(h, q):
        b = block_row(q)
        used = count[b]

        def panel(t):
            local = (cols[t, b] - first + blocks) & (blocks - 1)
            return scaled[h, jnp.where(t < used, local, SPAN * ROWS)]
        total = jnp.zeros((WIDE, TILE), jnp.float32)
        for t in range(0, SLOTS, 2):
            left = jnp.concatenate([panel(t), panel(t + 1)], axis=1)
            right = tiles[q, :, t * TILE:(t + 2) * TILE]
            total = total + lax.dot_general(left, right, NT, preferred_element_type=jnp.float32)
        total = total + scaled[h, REACH * ROWS + b].astype(jnp.float32)
        return (total * inv[pl.ds(REACH * ROWS + b, 1)]).astype(jnp.bfloat16)

    def aggregate_rows(h, s):
        for j in (2, 1, 3):
            def row(k, _, j=j):
                aggsend[h, j, k] = aggregate(h, j * GROUP + k)
                return 0
            lax.fori_loop(s * PAIRS, (s + 1) * PAIRS, row, 0, unroll=True)
            agg_copy(h, j, s).start()

        def row(k, _):
            aggrecv[k, h, chip] = aggregate(h, k)
            return 0
        lax.fori_loop(s * PAIRS, (s + 1) * PAIRS, row, 0, unroll=True)

    def finish(s):
        for h in range(HALVES):
            for j in (2, 1, 3):
                agg_copy(h, j, s).wait()
        for k in range(s * PAIRS, (s + 1) * PAIRS):
            values = aggrecv[k].reshape(HALVES * CHIPS * WIDE, TILE).astype(jnp.float32)
            peak_abs = jnp.max(jnp.abs(values))
            normalized = (values / (peak_abs + epsilon)).astype(jnp.bfloat16)
            mixed = lax.dot_general(normalized, order[...], TN, preferred_element_type=jnp.float32)
            out[k * TILE:(k + 1) * TILE] = jnp.maximum(mixed + bias[...], 0.0).astype(jnp.bfloat16)

    per_step = HALF // TOTAL
    for step in range(STEPS):
        transfer(step)
        if step < TOTAL:
            body = own_row if (step + 1) * per_step <= GROUP else more_row
            lax.fori_loop(step * per_step, (step + 1) * per_step, body, 0)
        if (step + 1) * per_step == GROUP:
            for d in offsets:
                degq_copy(d).start()
        if step == TOTAL // 2:
            for d in offsets:
                degq_copy(d).wait()
            for s in range(1, feats):
                degall_copy(s).start()
            degall[feat] = degq[...]
        if step == TOTAL - 2:
            for s in range(1, feats):
                degall_copy(s).wait()
            for f in range(feats):
                for d in range(SPAN):
                    inv[pl.ds(d * ROWS + f * GROUP, GROUP)] = lax.rsqrt(degall[f, d])
            own_copy.wait()
            for n in range(CHUNKS - 2):
                scale(n)
        if step == TOTAL:
            for n in range(CHUNKS - 2, CHUNKS):
                scale(n)
        if step >= TOTAL:
            aggregate_rows(0, step - TOTAL)
    for n in range(CHUNKS, TOTAL):
        scale(n)
    for s in range(SUBS):
        aggregate_rows(1, s)
    for s in range(SUBS):
        finish(s)

    @pl.when(outer)
    def _():
        for n in range(TOTAL):
            for source in (REACH, 3, PASS, 4):
                forward(outer_sends, source, n, wait=True)

    @pl.when(inner)
    def _():
        for n in range(TOTAL):
            for source in (REACH, 1, 4, 0):
                forward(inner_sends, source, n, wait=True)


def per_device(features, tile_cols, tile_count, edge_mask, weight, bias):
    feats = lax.axis_size("feat")
    smem = pl.BlockSpec(memory_space=pltpu.SMEM)
    vmem = pl.BlockSpec(memory_space=pltpu.VMEM)
    hbm = pl.BlockSpec(memory_space=pl.ANY)
    dma = pltpu.SemaphoreType.DMA
    return pl.pallas_call(
        kernel,
        out_shape=jax.ShapeDtypeStruct((GROUP * TILE, weight.shape[1]), jnp.bfloat16),
        in_specs=[hbm, hbm, smem, smem, vmem, vmem],
        out_specs=vmem,
        scratch_shapes=[
            pltpu.VMEM((STAGES, SLOTS, TILE, TILE), jnp.int32),
            pltpu.VMEM((HALF, TILE, SLOTS * TILE), jnp.bfloat16),
            pltpu.VMEM((CORES, SPAN + 1, PART, NODES), jnp.bfloat16),
            pltpu.VMEM((HALVES, SPAN * ROWS + 1, WIDE, TILE), jnp.bfloat16),
            pltpu.VMEM((SPAN * ROWS, TILE), jnp.float32),
            pltpu.VMEM((SPAN, GROUP, TILE), jnp.float32),
            pltpu.VMEM((feats, SPAN, GROUP, TILE), jnp.float32),
            pltpu.VMEM((HALVES, CHIPS, GROUP, WIDE, TILE), jnp.bfloat16),
            pltpu.VMEM((GROUP, HALVES, CHIPS, WIDE, TILE), jnp.bfloat16),
            pltpu.VMEM(weight.shape, jnp.bfloat16),
            dma((STAGES,)), dma, dma((SPAN + 1, TOTAL)), dma((SPAN + 1, TOTAL)),
            dma((SPAN, TOTAL)), dma((SPAN, TOTAL)),
            dma((SPAN,)), dma((SPAN,)), dma((feats,)), dma((feats,)),
            dma((HALVES, CHIPS, SUBS)), dma((HALVES, CHIPS, SUBS)),
        ],
        compiler_params=pltpu.CompilerParams(
            collective_id=0, has_side_effects=True, vmem_limit_bytes=60 * 1024 * 1024),
    )(features.T, edge_mask, tile_cols.T, tile_count, weight, bias.reshape(1, -1))


def solution(mesh):
    placed = (P("blk", "feat"), P("blk", None), P("blk"), P("blk", None, None, None), P(), P())
    return jax.shard_map(
        per_device, mesh=mesh, in_specs=placed, out_specs=P(("blk", "feat"), None), check_vma=False
    )
```

time: 82.8 us -> 72.2 us (0.87)
  Pallas kernels: 78 us -> 70.2 us
  other arithmetic: 1.35 us -> 0 us
    pallas_call x1, Pallas kernels: 78 us -> 70.2 us  [per_device(): pl.pallas_call(kernel, out_shape=jax.ShapeDtypeStruct((GROUP * TILE, weig...]
    select_n x1 -> x0, other arithmetic: 1.35 us -> none  [per_device(): idx = jnp.where(active, distance * ROWS + tile_cols % ROWS, SPAN * ROWS)]
    unnamed x2 -> x1, local copies, waits for them, and re-layouts: 2.65 us -> 1.87 us
where the time goes in v2:
time: 72.2 us; the launch traced here: 72.1 us
  Pallas kernels  70.2 us (97%)
  local copies, waits for them, and re-layouts  1.87 us (3%)
    pallas_call x1, Pallas kernels, per_device(): pl.pallas_call(kernel, out_shape=jax.ShapeDtypeStruct((GROUP * TILE, weig...  70.2 us
    unnamed x1, local copies, waits for them, and re-layouts  1.87 us

profile of v2, /device:TPU:2, one launch (start us, length us, event | category | flops | bytes accessed | tf_op | source)
XLA Modules:
  0.0 72.1 jit_solution(8768412217200379973)
XLA Ops:
  0.0 70.2 %shard_map.64 = bf16[1024,256]{1,0:T(8,128)(2,1)} custom-call(bf16[32,8192]{1,0:T(8,128)(2,1)} %bitcast.3, s32[64,16,128,128]{3,2,1,0:T(8,128)} %mask.1, s32[16,64]{1,0:T(8,128)} %bitcast.4, s32[64]{0:T(128)} %count.1, bf16[256,256]{1,0:T(8,128)(2,1)} %weight.1, f32[1,256]{1,0:T(1,128)} %bitcast.5), custom_call_target="tpu_custom_call" | custom-call | tf_op jit(solution)/shard_map/pallas_call | solution.py:362
  70.2 1.9 %copy.8 = bf16[1024,256]{1,0:T(8,128)(2,1)} copy(bf16[1024,256]{1,0:T(8,128)(2,1)} %shard_map.64) | data formatting | bytes 1048576

commit v3 on v1

v3 whole, which is shorter than its diff:
```python
import functools

import jax
import jax.numpy as jnp
from jax import lax
from jax.experimental import pallas as pl
from jax.experimental.pallas import tpu as pltpu
from jax.sharding import PartitionSpec as P

MESH = pl.DeviceIdType.MESH

TILE = 128
REACH = 2
SPAN = 2 * REACH + 1
epsilon = 1e-06

CORES = 2
ROWS = 64
SLOTS = 16
PART = 32
WIDE = CORES * PART
HALF = ROWS // CORES
GROUP = 8
CHIPS = 4
STAGES = 16
NODES = ROWS * TILE

CHUNKS = 4
BLOCKS = ROWS // CHUNKS
LANES = BLOCKS * TILE
PAIRS = 2
SUBS = GROUP // PAIRS

NN = (((1,), (0,)), ((), ()))
NT = (((1,), (1,)), ((), ()))
TN = (((0,), (0,)), ((), ()))


def kernel(
    ft, mask, cols, count, weight, bias, out,
    stage, tiles, raw, scaled, inv, degq, degall, aggsend, aggrecv, picks,
    stage_sem, own_sem, panel_send, panel_recv, pair_send, pair_recv,
    degq_send, degq_recv, degall_send, degall_recv, agg_send, agg_recv,
):
    blk = lax.axis_index("blk")
    feat = lax.axis_index("feat")
    owners = lax.axis_size("blk")
    feats = lax.axis_size("feat")
    chip, core = feat // CORES, feat % CORES
    partner = (blk, chip * CORES + 1 - core)

    def owner(d):
        return lax.rem(blk + d + owners, owners)

    def block_row(q):
        j, k = q // GROUP, q % GROUP
        return lax.rem(chip + j, CHIPS) * (CORES * GROUP) + core * GROUP + k

    def stage_copy(q):
        slot = q % STAGES
        return pltpu.make_async_copy(mask.at[block_row(q)], stage.at[slot], stage_sem.at[slot])

    for q in range(STAGES):
        stage_copy(q).start()
    own_copy = pltpu.make_async_copy(ft, raw.at[core, REACH], own_sem)
    own_copy.start()

    barrier = pltpu.get_barrier_semaphore()
    offsets = [d for d in range(-REACH, REACH + 1) if d != 0]
    peers = [(owner(d), feat) for d in offsets]
    peers += [(blk, lax.rem(feat + s, feats)) for s in range(1, feats)]
    for peer in peers:
        pl.semaphore_signal(barrier, inc=1, device_id=peer, device_id_type=MESH)
    pl.semaphore_wait(barrier, len(peers))

    def piece(n):
        return pl.ds(0, PART), pl.ds(n * LANES, LANES)

    def panel_copy(d, n):
        features, nodes = piece(n)
        sign = 1 if d > 0 else -1
        target = REACH + d
        source = target - sign
        src = ft.at[features, nodes] if source == REACH else raw.at[core, source, features, nodes]
        return pltpu.make_async_remote_copy(
            src_ref=src, dst_ref=raw.at[core, target, features, nodes],
            send_sem=panel_send.at[target, n], recv_sem=panel_recv.at[target, n],
            device_id=(owner(-sign), feat), device_id_type=MESH)

    def pair_copy(slot, n):
        features, nodes = piece(n)
        here = raw.at[core, slot, features, nodes]
        return pltpu.make_async_remote_copy(
            src_ref=ft.at[features, nodes] if slot == REACH else here, dst_ref=here,
            send_sem=pair_send.at[slot, n], recv_sem=pair_recv.at[slot, n],
            device_id=partner, device_id_type=MESH)

    def relay(d, n):
        panel_copy(d, n).wait_recv()
        if abs(d) < REACH:
            panel_copy(2 * d, n).start()
        pair_copy(REACH + d, n).start()

    for n in range(CHUNKS):
        for d in (-1, 1):
            panel_copy(d, n).start()
        if n == 0:
            for m in range(CHUNKS):
                pair_copy(REACH, m).start()

    scaled[SPAN * ROWS] = jnp.zeros((WIDE, TILE), jnp.bfloat16)

    first = (blk - REACH) * ROWS
    blocks = owners * ROWS

    def convert(q):
        slot = q % STAGES
        b = block_row(q)
        used = count[b]
        for t in range(SLOTS):
            local = (cols[t, b] - first + blocks) & (blocks - 1)
            picks[q, t] = jnp.where(t < used, local, SPAN * ROWS)
        stage_copy(q).wait()
        for t in range(SLOTS):
            tiles[q, t * TILE:(t + 1) * TILE] = stage[slot, t].astype(jnp.float32).astype(jnp.bfloat16).T

    def own_row(q, _):
        convert(q)
        n = count[block_row(q)]
        total = jnp.zeros((TILE, TILE), jnp.int32)
        for t in range(SLOTS):
            total = total + stage[q, t] * (t < n).astype(jnp.int32)
        total = total.astype(jnp.float32).astype(jnp.bfloat16)
        ones = jnp.ones((8, TILE), jnp.bfloat16)
        degree = 1.0 + lax.dot_general(ones, total, NT, preferred_element_type=jnp.float32)
        degq[REACH, pl.ds(q, 1)] = degree[0:1]
        stage_copy(q + STAGES).start()
        return 0

    def more_row(q, _):
        convert(q)

        @pl.when(q < HALF - STAGES)
        def _():
            stage_copy(q + STAGES).start()
        return 0

    def degq_copy(d):
        return pltpu.make_async_remote_copy(
            src_ref=degq.at[REACH], dst_ref=degq.at[REACH - d],
            send_sem=degq_send.at[REACH - d], recv_sem=degq_recv.at[REACH - d],
            device_id=(owner(d), feat), device_id_type=MESH)

    def degall_copy(s):
        return pltpu.make_async_remote_copy(
            src_ref=degq, dst_ref=degall.at[feat],
            send_sem=degall_send.at[s], recv_sem=degall_recv.at[s],
            device_id=(blk, lax.rem(feat + s, feats)), device_id_type=MESH)

    def scale(n, *ds):
        for d in ds:
            pair_copy(REACH + d, n).wait()
        for d in ds:
            slot = REACH + d

            def body(i, _, slot=slot):
                block = n * BLOCKS + i
                nodes = pl.ds(pl.multiple_of(block * TILE, TILE), TILE)
                factor = inv[pl.ds(slot * ROWS + block, 1)]
                for k in range(CORES):
                    values = raw[k, slot, :, nodes].astype(jnp.float32)
                    scaled[slot * ROWS + block, k * PART:(k + 1) * PART] = (values * factor).astype(jnp.bfloat16)
                return 0
            lax.fori_loop(0, BLOCKS, body, 0, unroll=4)

    def agg_copy(j, s):
        rows = pl.ds(s * PAIRS, PAIRS)
        return pltpu.make_async_remote_copy(
            src_ref=aggsend.at[j, rows], dst_ref=aggrecv.at[rows, chip],
            send_sem=agg_send.at[j, s], recv_sem=agg_recv.at[j, s],
            device_id=(blk, lax.rem(chip + j, CHIPS) * CORES + core), device_id_type=MESH)

    def aggregate_rows(s):
        def row(i, _):
            j, k = i // PAIRS, s * PAIRS + i % PAIRS
            q = j * GROUP + k
            b = block_row(q)
            left = jnp.concatenate([scaled[picks[q, t]] for t in range(SLOTS)], axis=1)
            total = lax.dot_general(left, tiles[q], NN, preferred_element_type=jnp.float32)
            total = total + scaled[REACH * ROWS + b].astype(jnp.float32)
            aggsend[j, k] = (total * inv[pl.ds(REACH * ROWS + b, 1)]).astype(jnp.bfloat16)
            return 0
        lax.fori_loop(0, CHIPS * PAIRS, row, 0, unroll=4)
        for j in (2, 1, 3):
            agg_copy(j, s).start()
        rows = pl.ds(s * PAIRS, PAIRS)
        aggrecv[rows, chip] = aggsend[0, rows]

    def finish(s):
        for j in (2, 1, 3):
            agg_copy(j, s).wait()
        for k in range(s * PAIRS, (s + 1) * PAIRS):
            values = aggrecv[k].reshape(CHIPS * WIDE, TILE).astype(jnp.float32)
            peak_abs = jnp.max(jnp.abs(values))
            normalized = (values / (peak_abs + epsilon)).astype(jnp.bfloat16)
            mixed = lax.dot_general(normalized, weight[...], TN, preferred_element_type=jnp.float32)
            out[k * TILE:(k + 1) * TILE] = jnp.maximum(mixed + bias[...], 0.0).astype(jnp.bfloat16)

    def near(n):
        for d in (-1, 1):
            relay(d, n)

    lax.fori_loop(0, GROUP, own_row, 0)
    for d in offsets:
        degq_copy(d).start()
    lax.fori_loop(GROUP, 12, more_row, 0)
    near(0)
    lax.fori_loop(12, 15, more_row, 0)
    for d in offsets:
        degq_copy(d).wait()
    for s in range(1, feats):
        degall_copy(s).start()
    degall[feat] = degq[...]
    lax.fori_loop(15, 19, more_row, 0)
    near(1)
    lax.fori_loop(19, 26, more_row, 0)
    near(2)
    lax.fori_loop(26, HALF, more_row, 0)
    near(3)
    for s in range(1, feats):
        degall_copy(s).wait()
    for f in range(feats):
        for d in range(SPAN):
            inv[pl.ds(d * ROWS + f * GROUP, GROUP)] = lax.rsqrt(degall[f, d])
    own_copy.wait()
    for n in range(CHUNKS):
        scale(n, 0, -1, 1)
        for d in (-2, 2):
            relay(d, n)
        if n > 0:
            scale(n - 1, -2, 2)
    scale(CHUNKS - 1, -2, 2)
    for s in range(SUBS):
        aggregate_rows(s)
        if s >= 2:
            finish(s - 2)
    for s in (SUBS - 2, SUBS - 1):
        finish(s)
    for n in range(CHUNKS):
        for d in offsets:
            panel_copy(d, n).wait_send()


def per_device(features, tile_cols, tile_count, edge_mask, weight, bias):
    feats = lax.axis_size("feat")
    smem = pl.BlockSpec(memory_space=pltpu.SMEM)
    vmem = pl.BlockSpec(memory_space=pltpu.VMEM)
    hbm = pl.BlockSpec(memory_space=pl.ANY)
    dma = pltpu.SemaphoreType.DMA
    return pl.pallas_call(
        kernel,
        out_shape=jax.ShapeDtypeStruct((GROUP * TILE, weight.shape[1]), jnp.bfloat16),
        in_specs=[hbm, hbm, smem, smem, vmem, vmem],
        out_specs=vmem,
        scratch_shapes=[
            pltpu.VMEM((STAGES, SLOTS, TILE, TILE), jnp.int32),
            pltpu.VMEM((HALF, SLOTS * TILE, TILE), jnp.bfloat16),
            pltpu.VMEM((CORES, SPAN, PART, NODES), jnp.bfloat16),
            pltpu.VMEM((SPAN * ROWS + 1, WIDE, TILE), jnp.bfloat16),
            pltpu.VMEM((SPAN * ROWS, TILE), jnp.float32),
            pltpu.VMEM((SPAN, GROUP, TILE), jnp.float32),
            pltpu.VMEM((feats, SPAN, GROUP, TILE), jnp.float32),
            pltpu.VMEM((CHIPS, GROUP, WIDE, TILE), jnp.bfloat16),
            pltpu.VMEM((GROUP, CHIPS, WIDE, TILE), jnp.bfloat16),
            pltpu.SMEM((HALF, SLOTS), jnp.int32),
            dma((STAGES,)), dma, dma((SPAN, CHUNKS)), dma((SPAN, CHUNKS)),
            dma((SPAN, CHUNKS)), dma((SPAN, CHUNKS)),
            dma((SPAN,)), dma((SPAN,)), dma((feats,)), dma((feats,)),
            dma((CHIPS, SUBS)), dma((CHIPS, SUBS)),
        ],
        compiler_params=pltpu.CompilerParams(
            collective_id=0, has_side_effects=True, vmem_limit_bytes=60 * 1024 * 1024),
    )(features.T, edge_mask, tile_cols.T, tile_count, weight, bias.reshape(1, -1))


def solution(mesh):
    placed = (P("blk", "feat"), P("blk", None), P("blk"), P("blk", None, None, None), P(), P())
    return jax.shard_map(
        per_device, mesh=mesh, in_specs=placed, out_specs=P(("blk", "feat"), None), check_vma=False
    )
```

time: 82.8 us -> 53.6 us (0.65)
  Pallas kernels: 78 us -> 51.6 us
  other arithmetic: 1.35 us -> 0 us
    pallas_call x1, Pallas kernels: 78 us -> 51.6 us  [per_device(): pl.pallas_call(kernel, out_shape=jax.ShapeDtypeStruct((GROUP * TILE, weig...]
    select_n x1 -> x0, other arithmetic: 1.35 us -> none  [per_device(): idx = jnp.where(active, distance * ROWS + tile_cols % ROWS, SPAN * ROWS)]
    unnamed x2 -> x1, local copies, waits for them, and re-layouts: 2.65 us -> 1.87 us
where the time goes in v3:
time: 53.6 us; the launch traced here: 53.5 us
  Pallas kernels  51.6 us (96%)
  local copies, waits for them, and re-layouts  1.87 us (3%)
    pallas_call x1, Pallas kernels, per_device(): pl.pallas_call(kernel, out_shape=jax.ShapeDtypeStruct((GROUP * TILE, weig...  51.6 us
    unnamed x1, local copies, waits for them, and re-layouts  1.87 us

profile of v3, /device:TPU:2, one launch (start us, length us, event | category | flops | bytes accessed | tf_op | source)
XLA Modules:
  0.0 53.5 jit_solution(14051630281142198241)
XLA Ops:
  0.0 51.6 %shard_map.64 = bf16[1024,256]{1,0:T(8,128)(2,1)} custom-call(bf16[32,8192]{1,0:T(8,128)(2,1)} %bitcast.3, s32[64,16,128,128]{3,2,1,0:T(8,128)} %mask.1, s32[16,64]{1,0:T(8,128)} %bitcast.4, s32[64]{0:T(128)} %count.1, bf16[256,256]{1,0:T(8,128)(2,1)} %weight.1, f32[1,256]{1,0:T(1,128)} %bitcast.5), custom_call_target="tpu_custom_call" | custom-call | tf_op jit(solution)/shard_map/pallas_call | solution.py:260
  51.6 1.9 %copy.8 = bf16[1024,256]{1,0:T(8,128)(2,1)} copy(bf16[1024,256]{1,0:T(8,128)(2,1)} %shard_map.64) | data formatting | bytes 1048576

commit v4 on v3

--- a/solution.py
+++ b/solution.py
@@ -18,16 +18,21 @@
 ROWS = 64
 SLOTS = 16
 PART = 32
-WIDE = CORES * PART
+HALVES = 2
+SUB = PART // HALVES
+WIDE = CORES * SUB
 HALF = ROWS // CORES
 GROUP = 8
 CHIPS = 4
 STAGES = 16
+DEGREES = 1
 NODES = ROWS * TILE
 
-CHUNKS = 4
-BLOCKS = ROWS // CHUNKS
+CUTS = 2
+CHUNKS = HALVES * CUTS
+BLOCKS = ROWS // CUTS
 LANES = BLOCKS * TILE
+AHEAD = 4
 PAIRS = 2
 SUBS = GROUP // PAIRS
 
@@ -37,9 +42,9 @@
 
 
 def kernel(
-    ft, mask, cols, count, weight, bias, out,
-    stage, tiles, raw, scaled, inv, degq, degall, aggsend, aggrecv, picks,
-    stage_sem, own_sem, panel_send, panel_recv, pair_send, pair_recv,
+    ft, mask, cols_in, count_in, weight_in, bias_in, out_hbm,
+    cols, count, weight, bias, out, stage, tiles, raw, scaled, inv, degq, degall, aggsend, aggrecv, picks, order,
+    small_sem, out_sem, stage_sem, own_sem, panel_send, panel_recv, pair_send, pair_recv,
     degq_send, degq_recv, degall_send, degall_recv, agg_send, agg_recv,
 ):
     blk = lax.axis_index("blk")
@@ -60,21 +65,29 @@
         slot = q % STAGES
         return pltpu.make_async_copy(mask.at[block_row(q)], stage.at[slot], stage_sem.at[slot])
 
-    for q in range(STAGES):
-        stage_copy(q).start()
-    own_copy = pltpu.make_async_copy(ft, raw.at[core, REACH], own_sem)
-    own_copy.start()
-
     barrier = pltpu.get_barrier_semaphore()
     offsets = [d for d in range(-REACH, REACH + 1) if d != 0]
     peers = [(owner(d), feat) for d in offsets]
     peers += [(blk, lax.rem(feat + s, feats)) for s in range(1, feats)]
     for peer in peers:
         pl.semaphore_signal(barrier, inc=1, device_id=peer, device_id_type=MESH)
+    small = [
+        pltpu.make_async_copy(source, target, small_sem.at[i]) for i, (source, target) in enumerate(
+            ((cols_in, cols), (count_in, count), (weight_in, weight), (bias_in, bias)))]
+    for copy in small[:2]:
+        copy.start()
+    for q in range(STAGES):
+        stage_copy(q).start()
+    own_copy = pltpu.make_async_copy(ft, raw.at[core, REACH], own_sem)
+    own_copy.start()
+    for copy in small[2:]:
+        copy.start()
+    for copy in small[:2]:
+        copy.wait()
     pl.semaphore_wait(barrier, len(peers))
 
     def piece(n):
-        return pl.ds(0, PART), pl.ds(n * LANES, LANES)
+        return pl.ds(n // CUTS * SUB, SUB), pl.ds(n % CUTS * LANES, LANES)
 
     def panel_copy(d, n):
         features, nodes = piece(n)
@@ -101,14 +114,17 @@
             panel_copy(2 * d, n).start()
         pair_copy(REACH + d, n).start()
 
-    for n in range(CHUNKS):
+    def send_own(n):
         for d in (-1, 1):
             panel_copy(d, n).start()
-        if n == 0:
-            for m in range(CHUNKS):
-                pair_copy(REACH, m).start()
-
-    scaled[SPAN * ROWS] = jnp.zeros((WIDE, TILE), jnp.bfloat16)
+
+    for n in range(AHEAD):
+        send_own(n)
+    for n in range(CHUNKS):
+        pair_copy(REACH, n).start()
+
+    for h in range(HALVES):
+        scaled[h, SPAN * ROWS] = jnp.zeros((WIDE, TILE), jnp.bfloat16)
 
     first = (blk - REACH) * ROWS
     blocks = owners * ROWS
@@ -158,125 +174,160 @@
             device_id=(blk, lax.rem(feat + s, feats)), device_id_type=MESH)
 
     def scale(n, *ds):
+        h = n // CUTS
         for d in ds:
             pair_copy(REACH + d, n).wait()
         for d in ds:
             slot = REACH + d
 
             def body(i, _, slot=slot):
-                block = n * BLOCKS + i
+                block = n % CUTS * BLOCKS + i
                 nodes = pl.ds(pl.multiple_of(block * TILE, TILE), TILE)
                 factor = inv[pl.ds(slot * ROWS + block, 1)]
                 for k in range(CORES):
-                    values = raw[k, slot, :, nodes].astype(jnp.float32)
-                    scaled[slot * ROWS + block, k * PART:(k + 1) * PART] = (values * factor).astype(jnp.bfloat16)
+                    values = raw[k, slot, h * SUB:(h + 1) * SUB, nodes].astype(jnp.float32)
+                    scaled[h, slot * ROWS + block, k * SUB:(k + 1) * SUB] = (values * factor).astype(jnp.bfloat16)
                 return 0
             lax.fori_loop(0, BLOCKS, body, 0, unroll=4)
 
-    def agg_copy(j, s):
+    def agg_copy(h, j, s):
         rows = pl.ds(s * PAIRS, PAIRS)
         return pltpu.make_async_remote_copy(
-            src_ref=aggsend.at[j, rows], dst_ref=aggrecv.at[rows, chip],
-            send_sem=agg_send.at[j, s], recv_sem=agg_recv.at[j, s],
+            src_ref=aggsend.at[h, j, rows], dst_ref=aggrecv.at[rows, h, chip],
+            send_sem=agg_send.at[h, j, s], recv_sem=agg_recv.at[h, j, s],
             device_id=(blk, lax.rem(chip + j, CHIPS) * CORES + core), device_id_type=MESH)
 
-    def aggregate_rows(s):
+    def aggregate_rows(h, s):
         def row(i, _):
             j, k = i // PAIRS, s * PAIRS + i % PAIRS
             q = j * GROUP + k
             b = block_row(q)
-            left = jnp.concatenate([scaled[picks[q, t]] for t in range(SLOTS)], axis=1)
+            left = jnp.concatenate([scaled[h, picks[q, t]] for t in range(SLOTS)], axis=1)
             total = lax.dot_general(left, tiles[q], NN, preferred_element_type=jnp.float32)
-            total = total + scaled[REACH * ROWS + b].astype(jnp.float32)
-            aggsend[j, k] = (total * inv[pl.ds(REACH * ROWS + b, 1)]).astype(jnp.bfloat16)
+            total = total + scaled[h, REACH * ROWS + b].astype(jnp.float32)
+            aggsend[h, j, k] = (total * inv[pl.ds(REACH * ROWS + b, 1)]).astype(jnp.bfloat16)
             return 0
-        lax.fori_loop(0, CHIPS * PAIRS, row, 0, unroll=4)
+        lax.fori_loop(0, CHIPS * PAIRS, row, 0, unroll=8)
         for j in (2, 1, 3):
-            agg_copy(j, s).start()
+            agg_copy(h, j, s).start()
         rows = pl.ds(s * PAIRS, PAIRS)
-        aggrecv[rows, chip] = aggsend[0, rows]
+        aggrecv[rows, h, chip] = aggsend[h, 0, rows]
+
+    def out_copy(s):
+        rows = pl.ds(s * PAIRS * TILE, PAIRS * TILE)
+        return pltpu.make_async_copy(out.at[rows], out_hbm.at[rows], out_sem.at[s])
 
     def finish(s):
-        for j in (2, 1, 3):
-            agg_copy(j, s).wait()
+        for h in range(HALVES):
+            for j in (2, 1, 3):
+                agg_copy(h, j, s).wait()
         for k in range(s * PAIRS, (s + 1) * PAIRS):
-            values = aggrecv[k].reshape(CHIPS * WIDE, TILE).astype(jnp.float32)
+            values = aggrecv[k].reshape(HALVES * CHIPS * WIDE, TILE).astype(jnp.float32)
             peak_abs = jnp.max(jnp.abs(values))
             normalized = (values / (peak_abs + epsilon)).astype(jnp.bfloat16)
-            mixed = lax.dot_general(normalized, weight[...], TN, preferred_element_type=jnp.float32)
+            mixed = lax.dot_general(normalized, order[...], TN, preferred_element_type=jnp.float32)
             out[k * TILE:(k + 1) * TILE] = jnp.maximum(mixed + bias[...], 0.0).astype(jnp.bfloat16)
 
     def near(n):
         for d in (-1, 1):
             relay(d, n)
+        if n + AHEAD < CHUNKS:
+            send_own(n + AHEAD)
+
+    def far(n):
+        for d in (-2, 2):
+            relay(d, n)
 
     lax.fori_loop(0, GROUP, own_row, 0)
     for d in offsets:
         degq_copy(d).start()
-    lax.fori_loop(GROUP, 12, more_row, 0)
-    near(0)
-    lax.fori_loop(12, 15, more_row, 0)
-    for d in offsets:
-        degq_copy(d).wait()
-    for s in range(1, feats):
-        degall_copy(s).start()
-    degall[feat] = degq[...]
-    lax.fori_loop(15, 19, more_row, 0)
-    near(1)
-    lax.fori_loop(19, 26, more_row, 0)
-    near(2)
-    lax.fori_loop(26, HALF, more_row, 0)
-    near(3)
+    done = GROUP
+    for n in range(CHUNKS):
+        near(n)
+        if n == DEGREES:
+            for d in offsets:
+                degq_copy(d).wait()
+            for s in range(1, feats):
+                degall_copy(s).start()
+            degall[feat] = degq[...]
+        more = (HALF - GROUP) * (n + 1) // CHUNKS + GROUP
+        lax.fori_loop(done, more, more_row, 0)
+        done = more
+    far(0)
     for s in range(1, feats):
         degall_copy(s).wait()
     for f in range(feats):
         for d in range(SPAN):
             inv[pl.ds(d * ROWS + f * GROUP, GROUP)] = lax.rsqrt(degall[f, d])
     own_copy.wait()
-    for n in range(CHUNKS):
-        scale(n, 0, -1, 1)
-        for d in (-2, 2):
-            relay(d, n)
-        if n > 0:
-            scale(n - 1, -2, 2)
-    scale(CHUNKS - 1, -2, 2)
+    scale(0, 0, -1, 1)
+    far(1)
+    scale(1, 0, -1, 1)
+    scale(0, -2, 2)
+    scale(1, -2, 2)
+    aggregate_rows(0, 0)
+    scale(2, 0, -1, 1)
+    aggregate_rows(0, 1)
+    far(2)
+    scale(3, 0, -1, 1)
+    aggregate_rows(0, 2)
+    scale(2, -2, 2)
+    for copy in small[2:]:
+        copy.wait()
+    for x in range(CHIPS):
+        for c in range(CORES):
+            for h in range(HALVES):
+                source = (x * CORES + c) * PART + h * SUB
+                target = (h * CHIPS + x) * WIDE + c * SUB
+                order[target:target + SUB] = weight[source:source + SUB]
+    aggregate_rows(0, 3)
+    far(3)
+    scale(3, -2, 2)
     for s in range(SUBS):
-        aggregate_rows(s)
+        aggregate_rows(1, s)
         if s >= 2:
             finish(s - 2)
+            out_copy(s - 2).start()
     for s in (SUBS - 2, SUBS - 1):
         finish(s)
+        out_copy(s).start()
     for n in range(CHUNKS):
         for d in offsets:
             panel_copy(d, n).wait_send()
+    for s in range(SUBS):
+        out_copy(s).wait()
 
 
 def per_device(features, tile_cols, tile_count, edge_mask, weight, bias):
     feats = lax.axis_size("feat")
-    smem = pl.BlockSpec(memory_space=pltpu.SMEM)
-    vmem = pl.BlockSpec(memory_space=pltpu.VMEM)
     hbm = pl.BlockSpec(memory_space=pl.ANY)
     dma = pltpu.SemaphoreType.DMA
     return pl.pallas_call(
         kernel,
         out_shape=jax.ShapeDtypeStruct((GROUP * TILE, weight.shape[1]), jnp.bfloat16),
-        in_specs=[hbm, hbm, smem, smem, vmem, vmem],
-        out_specs=vmem,
+        in_specs=[hbm] * 6,
+        out_specs=hbm,
         scratch_shapes=[
+            pltpu.SMEM((SLOTS, ROWS), jnp.int32),
+            pltpu.SMEM((ROWS,), jnp.int32),
+            pltpu.VMEM(weight.shape, jnp.bfloat16),
+            pltpu.VMEM((1, weight.shape[1]), jnp.float32),
+            pltpu.VMEM((GROUP * TILE, weight.shape[1]), jnp.bfloat16),
             pltpu.VMEM((STAGES, SLOTS, TILE, TILE), jnp.int32),
             pltpu.VMEM((HALF, SLOTS * TILE, TILE), jnp.bfloat16),
             pltpu.VMEM((CORES, SPAN, PART, NODES), jnp.bfloat16),
-            pltpu.VMEM((SPAN * ROWS + 1, WIDE, TILE), jnp.bfloat16),
+            pltpu.VMEM((HALVES, SPAN * ROWS + 1, WIDE, TILE), jnp.bfloat16),
             pltpu.VMEM((SPAN * ROWS, TILE), jnp.float32),
             pltpu.VMEM((SPAN, GROUP, TILE), jnp.float32),
             pltpu.VMEM((feats, SPAN, GROUP, TILE), jnp.float32),
-            pltpu.VMEM((CHIPS, GROUP, WIDE, TILE), jnp.bfloat16),
-            pltpu.VMEM((GROUP, CHIPS, WIDE, TILE), jnp.bfloat16),
+            pltpu.VMEM((HALVES, CHIPS, GROUP, WIDE, TILE), jnp.bfloat16),
+            pltpu.VMEM((GROUP, HALVES, CHIPS, WIDE, TILE), jnp.bfloat16),
             pltpu.SMEM((HALF, SLOTS), jnp.int32),
-            dma((STAGES,)), dma, dma((SPAN, CHUNKS)), dma((SPAN, CHUNKS)),
+            pltpu.VMEM(weight.shape, jnp.bfloat16),
+            dma((4,)), dma((SUBS,)), dma((STAGES,)), dma, dma((SPAN, CHUNKS)), dma((SPAN, CHUNKS)),
             dma((SPAN, CHUNKS)), dma((SPAN, CHUNKS)),
             dma((SPAN,)), dma((SPAN,)), dma((feats,)), dma((feats,)),
-            dma((CHIPS, SUBS)), dma((CHIPS, SUBS)),
+            dma((HALVES, CHIPS, SUBS)), dma((HALVES, CHIPS, SUBS)),
         ],
         compiler_params=pltpu.CompilerParams(
             collective_id=0, has_side_effects=True, vmem_limit_bytes=60 * 1024 * 1024),

time: 53.6 us -> 50.5 us (0.942)
  Pallas kernels: 51.6 us -> 48.3 us
    pallas_call x1, Pallas kernels: 51.6 us -> 48.3 us  [per_device(): pl.pallas_call(kernel, out_shape=jax.ShapeDtypeStruct((GROUP * TILE, weig...]
where the time goes in v4:
time: 50.5 us; the launch traced here: 50.2 us
  Pallas kernels  48.3 us (96%)
  local copies, waits for them, and re-layouts  1.87 us (4%)
    pallas_call x1, Pallas kernels, per_device(): pl.pallas_call(kernel, out_shape=jax.ShapeDtypeStruct((GROUP * TILE, weig...  48.3 us
    unnamed x1, local copies, waits for them, and re-layouts  1.87 us

profile of v4, /device:TPU:2, one launch (start us, length us, event | category | flops | bytes accessed | tf_op | source)
XLA Modules:
  0.0 50.2 jit_solution(7877751136241020552)
XLA Ops:
  0.0 48.3 %shard_map.64 = bf16[1024,256]{1,0:T(8,128)(2,1)} custom-call(bf16[32,8192]{1,0:T(8,128)(2,1)} %bitcast.3, s32[64,16,128,128]{3,2,1,0:T(8,128)} %mask.1, s32[16,64]{1,0:T(8,128)} %bitcast.4, s32[64]{0:T(128)} %count_in.1, bf16[256,256]{1,0:T(8,128)(2,1)} %weight_in.1, f32[1,256]{1,0:T(1,128)} %bitcast.5), custom_call_target="tpu_custom_call" | custom-call | tf_op jit(solution)/shard_map/pallas_call | solution.py:305
  48.3 1.9 %copy.8 = bf16[1024,256]{1,0:T(8,128)(2,1)} copy(bf16[1024,256]{1,0:T(8,128)(2,1)} %shard_map.64) | data formatting | bytes 1048576

commit v5 on v4

--- a/solution.py
+++ b/solution.py
@@ -24,7 +24,7 @@
 HALF = ROWS // CORES
 GROUP = 8
 CHIPS = 4
-STAGES = 16
+STAGES = 8
 DEGREES = 1
 NODES = ROWS * TILE
 
@@ -207,9 +207,10 @@
             total = total + scaled[h, REACH * ROWS + b].astype(jnp.float32)
             aggsend[h, j, k] = (total * inv[pl.ds(REACH * ROWS + b, 1)]).astype(jnp.bfloat16)
             return 0
-        lax.fori_loop(0, CHIPS * PAIRS, row, 0, unroll=8)
+        lax.fori_loop(PAIRS, CHIPS * PAIRS, row, 0, unroll=True)
         for j in (2, 1, 3):
             agg_copy(h, j, s).start()
+        lax.fori_loop(0, PAIRS, row, 0, unroll=True)
         rows = pl.ds(s * PAIRS, PAIRS)
         aggrecv[rows, h, chip] = aggsend[h, 0, rows]
 
@@ -280,8 +281,8 @@
                 source = (x * CORES + c) * PART + h * SUB
                 target = (h * CHIPS + x) * WIDE + c * SUB
                 order[target:target + SUB] = weight[source:source + SUB]
+    far(3)
     aggregate_rows(0, 3)
-    far(3)
     scale(3, -2, 2)
     for s in range(SUBS):
         aggregate_rows(1, s)

time: 50.5 us -> 49.8 us (0.986)
  Pallas kernels: 48.3 us -> 47.2 us
    pallas_call x1, Pallas kernels: 48.3 us -> 47.2 us  [per_device(): pl.pallas_call(kernel, out_shape=jax.ShapeDtypeStruct((GROUP * TILE, weig...]
where the time goes in v5:
time: 49.8 us; the launch traced here: 49.1 us
  Pallas kernels  47.2 us (95%)
  local copies, waits for them, and re-layouts  1.87 us (4%)
    pallas_call x1, Pallas kernels, per_device(): pl.pallas_call(kernel, out_shape=jax.ShapeDtypeStruct((GROUP * TILE, weig...  47.2 us
    unnamed x1, local copies, waits for them, and re-layouts  1.87 us

profile of v5, /device:TPU:2, one launch (start us, length us, event | category | flops | bytes accessed | tf_op | source)
XLA Modules:
  0.0 49.1 jit_solution(11284534312008333421)
XLA Ops:
  0.0 47.2 %shard_map.64 = bf16[1024,256]{1,0:T(8,128)(2,1)} custom-call(bf16[32,8192]{1,0:T(8,128)(2,1)} %bitcast.3, s32[64,16,128,128]{3,2,1,0:T(8,128)} %mask.1, s32[16,64]{1,0:T(8,128)} %bitcast.4, s32[64]{0:T(128)} %count_in.1, bf16[256,256]{1,0:T(8,128)(2,1)} %weight_in.1, f32[1,256]{1,0:T(1,128)} %bitcast.5), custom_call_target="tpu_custom_call" | custom-call | tf_op jit(solution)/shard_map/pallas_call | solution.py:306
  47.2 1.9 %copy.8 = bf16[1024,256]{1,0:T(8,128)(2,1)} copy(bf16[1024,256]{1,0:T(8,128)(2,1)} %shard_map.64) | data formatting | bytes 1048576

commit v6 on v5

--- a/solution.py
+++ b/solution.py
@@ -268,8 +268,8 @@
     scale(1, -2, 2)
     aggregate_rows(0, 0)
     scale(2, 0, -1, 1)
+    far(2)
     aggregate_rows(0, 1)
-    far(2)
     scale(3, 0, -1, 1)
     aggregate_rows(0, 2)
     scale(2, -2, 2)

time: 49.8 us -> 50.2 us (level)
  Pallas kernels: 47.2 us -> 48 us
    pallas_call x1, Pallas kernels: 47.2 us -> 48 us  [per_device(): pl.pallas_call(kernel, out_shape=jax.ShapeDtypeStruct((GROUP * TILE, weig...]
where the time goes in v6:
time: 50.2 us; the launch traced here: 49.8 us
  Pallas kernels  48 us (96%)
  local copies, waits for them, and re-layouts  1.87 us (4%)
    pallas_call x1, Pallas kernels, per_device(): pl.pallas_call(kernel, out_shape=jax.ShapeDtypeStruct((GROUP * TILE, weig...  48 us
    unnamed x1, local copies, waits for them, and re-layouts  1.87 us

profile of v6, /device:TPU:2, one launch (start us, length us, event | category | flops | bytes accessed | tf_op | source)
XLA Modules:
  0.0 49.8 jit_solution(2108224135230337593)
XLA Ops:
  0.0 48.0 %shard_map.64 = bf16[1024,256]{1,0:T(8,128)(2,1)} custom-call(bf16[32,8192]{1,0:T(8,128)(2,1)} %bitcast.3, s32[64,16,128,128]{3,2,1,0:T(8,128)} %mask.1, s32[16,64]{1,0:T(8,128)} %bitcast.4, s32[64]{0:T(128)} %count_in.1, bf16[256,256]{1,0:T(8,128)(2,1)} %weight_in.1, f32[1,256]{1,0:T(1,128)} %bitcast.5), custom_call_target="tpu_custom_call" | custom-call | tf_op jit(solution)/shard_map/pallas_call | solution.py:306
  48.0 1.9 %copy.8 = bf16[1024,256]{1,0:T(8,128)(2,1)} copy(bf16[1024,256]{1,0:T(8,128)(2,1)} %shard_map.64) | data formatting | bytes 1048576
